TPU v7x, 32 devices: a whole 2x2x4 slice. The times are simulated.
32 devices in a mesh: group: 2 (over y), context: 4 (over z), tensor: 2 (over x), strand: 2 (over core).
Axes of the slice: x: 2, y: 2, z: 4, core: 2. Of those that a mesh axis runs over, the one named last changes fastest.
Arguments:
- trunk_rows: bfloat16 [2, 2048, 1536], P('strand', ('group', 'context'), 'tensor'), parts along dimension 1, may hold values from -6 to 6
- skip_mid: bfloat16 [2, 4096, 1536], P('strand', ('group', 'context'), 'tensor'), parts along dimension 1, may hold values from -6 to 6
- skip_fine: bfloat16 [2, 8192, 1536], P('strand', ('group', 'context'), 'tensor'), parts along dimension 1, may hold values from -6 to 6
- coarse_mid: bfloat16 [1536, 1536], P(None, 'tensor'), may hold values from -0.15625 to 0.15625
- lateral_mid: bfloat16 [1536, 1536], P(None, 'tensor'), may hold values from -0.15625 to 0.15625
- gain_mid: float32 [1536], P('tensor'), may hold values from 0.1 to 1.9
- shift_mid: float32 [1536], P('tensor'), may hold values from -0.5 to 0.5
- depth_mid: bfloat16 [3, 1536], P(None, 'tensor'), may hold values from -3.5 to 3.5
- mixing_mid: bfloat16 [1536, 1536], P(None, 'tensor'), may hold values from -0.15625 to 0.15625
- coarse_fine: bfloat16 [1536, 1536], P(None, 'tensor'), may hold values from -0.15625 to 0.15625
- lateral_fine: bfloat16 [1536, 1536], P(None, 'tensor'), may hold values from -0.15625 to 0.15625
- gain_fine: float32 [1536], P('tensor'), may hold values from 0.1 to 1.9
- shift_fine: float32 [1536], P('tensor'), may hold values from -0.5 to 0.5
- depth_fine: bfloat16 [3, 1536], P(None, 'tensor'), may hold values from -3.5 to 3.5
- mixing_fine: bfloat16 [1536, 1536], P(None, 'tensor'), may hold values from -0.15625 to 0.15625
- head_weight: bfloat16 [1536, 4096], P(None, 'tensor'), may hold values from -0.15625 to 0.15625
Outputs:
- averaged: bfloat16 [2, 8192, 4096], P('strand', ('group', 'context'), 'tensor'), parts along dimension 1
There are 2 independent parts, one for each index of `group`. A program takes and returns all parts, laid end to end along the dimension named above; an argument that names none is the same for every part. Nothing has to cross between parts.
All inputs are finite; a program needn't handle non-finite values.
Results may differ from a plain program's by a relative error of at most 0.0085.
Values may be sent and summed in bfloat16 or wider, within the bound.
A program may use at most 128 MiB of HBM per device.

v0:
```python
import jax
import jax.numpy as jnp
from jax import lax
from jax.sharding import PartitionSpec as P


def with_halo(block, sides, width):
    for axis, dim in sides:
        count = lax.axis_size(axis)
        forward = [(i, i + 1) for i in range(count - 1)]
        backward = [(target, source) for source, target in forward]
        low = lax.ppermute(
            lax.slice_in_dim(block, block.shape[dim] - width, None, axis=dim), axis, forward
        )
        high = lax.ppermute(lax.slice_in_dim(block, 0, width, axis=dim), axis, backward)
        block = jnp.concatenate([low, block, high], axis=dim)
    return block


def from_partner(value, axis, apart):
    mask = 2**apart
    pairs = [(source, source ^ mask) for source in range(lax.axis_size(axis))]
    return lax.ppermute(value, axis, pairs)


def contract(portion, weight):
    return jnp.dot(portion, weight, preferred_element_type=jnp.float32)


def upsample_section(coarse, lateral_in, coarse_weight, lateral_weight, gain, shift, depth, mixing):
    lifted = contract(lax.all_gather(coarse, "tensor", axis=1, tiled=True), coarse_weight)
    skipped = contract(lax.all_gather(lateral_in, "tensor", axis=1, tiled=True), lateral_weight)
    upsampled = jnp.repeat(lifted, 2, axis=0)
    active = jax.nn.gelu(gain * (upsampled + skipped) + shift).astype(jnp.bfloat16)
    padded = with_halo(active, (("context", 0),), 1).astype(jnp.float32)
    kernel_taps = depth.astype(jnp.float32)
    depthwise = (
        kernel_taps[0] * padded[:-2] + kernel_taps[1] * padded[1:-1] + kernel_taps[2] * padded[2:]
    ).astype(jnp.bfloat16)
    mixed_out = contract(lax.all_gather(depthwise, "tensor", axis=1, tiled=True), mixing)
    return mixed_out.astype(jnp.bfloat16)


def flip_tracks(values, total_tracks):
    row_count, track_count = values.shape
    swapped = values.reshape(row_count, track_count // 2, 2)[:, :, ::-1].reshape(
        row_count, track_count
    )
    track_index = lax.axis_index("tensor") * track_count + jnp.arange(track_count)
    return jnp.where((track_index < total_tracks // 2)[None, :], swapped, values)


def on_device(
    trunk_rows,
    skip_mid,
    skip_fine,
    coarse_mid,
    lateral_mid,
    gain_mid,
    shift_mid,
    depth_mid,
    mixing_mid,
    coarse_fine,
    lateral_fine,
    gain_fine,
    shift_fine,
    depth_fine,
    mixing_fine,
    head_weight,
):
    hidden_mid = upsample_section(
        trunk_rows[0],
        skip_mid[0],
        coarse_mid,
        lateral_mid,
        gain_mid,
        shift_mid,
        depth_mid,
        mixing_mid,
    )
    hidden_fine = upsample_section(
        hidden_mid,
        skip_fine[0],
        coarse_fine,
        lateral_fine,
        gain_fine,
        shift_fine,
        depth_fine,
        mixing_fine,
    )
    total_tracks = head_weight.shape[1] * lax.axis_size("tensor")
    slab_count = lax.axis_size("context")
    row_count, width = hidden_fine.shape
    block_rows = row_count // slab_count
    crossed = from_partner(hidden_fine, "strand", 0)
    spread_rows = lax.all_to_all(crossed, "context", split_axis=0, concat_axis=0, tiled=True)
    blocks = spread_rows.reshape(slab_count, block_rows, width)
    reordered = jnp.flip(blocks, (0, 1)).reshape(row_count, width)
    returned = lax.all_to_all(reordered, "context", split_axis=0, concat_axis=0, tiled=True)
    partner = jnp.flip(returned.reshape(slab_count, block_rows, width), 0).reshape(row_count, width)
    own_logits = contract(lax.all_gather(hidden_fine, "tensor", axis=1, tiled=True), head_weight)
    partner_logits = contract(lax.all_gather(partner, "tensor", axis=1, tiled=True), head_weight)
    predicted = jax.nn.softplus(own_logits).astype(jnp.bfloat16)
    mirrored = flip_tracks(jax.nn.softplus(partner_logits).astype(jnp.bfloat16), total_tracks)
    averaged = (0.5 * (predicted.astype(jnp.float32) + mirrored.astype(jnp.float32))).astype(
        jnp.bfloat16
    )
    return averaged[None]


def solution(mesh):
    in_specs = (
        P("strand", ("group", "context"), "tensor"),
        P("strand", ("group", "context"), "tensor"),
        P("strand", ("group", "context"), "tensor"),
        P(None, "tensor"),
        P(None, "tensor"),
        P("tensor"),
        P("tensor"),
        P(None, "tensor"),
        P(None, "tensor"),
        P(None, "tensor"),
        P(None, "tensor"),
        P("tensor"),
        P("tensor"),
        P(None, "tensor"),
        P(None, "tensor"),
        P(None, "tensor"),
    )
    out_specs = P("strand", ("group", "context"), "tensor")
    return jax.shard_map(
        on_device, mesh=mesh, in_specs=in_specs, out_specs=out_specs, check_vma=False
    )
```

profile of v0, /device:TPU:0, one launch (start us, length us, event | category | flops | bytes accessed | tf_op | source)
XLA Modules:
  0.0 481.4 jit_solution(6832214556921300199)
XLA Ops:
  7.3 13.0 %all-gather = bf16[1,256,1536]{2,1,0:T(8,128)(2,1)S(1)} all-gather(bf16[1,256,768]{2,1,0:T(8,128)(2,1)} %param.16), channel_id=2, replica_groups=mesh['group'=2,'context'=4,'tensor'=2,'strand'=2] {'tensor'}, dimensions={2}, use_global_device_ids=true | all-gather | bytes 1179648 | tf_op jit(solution)/shard_map/all_gather | solution.py:31
  20.3 2.5 fusion.33
  24.5 3.1 reshape.38
  27.6 11.2 %all-gather.21.cloned.1.call-done = bf16[1,512,1536]{2,1,0:T(8,128)(2,1)} async-done(((bf16[1,512,768]{2,1,0:T(8,128)(2,1)}), bf16[1,512,1536]{2,1,0:T(8,128)(2,1)}) %all-gather.21.cloned.1.call-update) | async-done | bytes 1572880 | tf_op jit(solution)/shard_map/all_gather | solution.py:32
  38.8 4.3 fusion.25
  43.2 3.4 collective-permute-start
  47.9 4.1 collective-permute-done.1
  53.7 26.4 %all-gather.11.cloned.1.call-done = bf16[512,1536]{1,0:T(8,128)(2,1)} async-done(((bf16[512,768]{1,0:T(8,128)(2,1)}), bf16[512,1536]{1,0:T(8,128)(2,1)}) %all-gather.11.cloned.1.call-update) | async-done | bytes 1572880 | tf_op jit(solution)/shard_map/all_gather | solution.py:40
  80.1 4.4 convolution_convert_fusion.1
  85.4 26.5 %all-gather.13.cloned.1.call-done = bf16[512,1536]{1,0:T(8,128)(2,1)} async-done(((bf16[512,768]{1,0:T(8,128)(2,1)}), bf16[512,1536]{1,0:T(8,128)(2,1)}) %all-gather.13.cloned.1.call-update) | async-done | bytes 1572880 | tf_op jit(solution)/shard_map/all_gather | solution.py:31
  111.9 3.5 fusion.37
  115.4 2.7 broadcast_in_dim.23
  118.2 5.7 %reshape.39 = f32[1024,768]{1,0:T(8,128)} reshape(f32[512,2,768]{2,1,0:T(2,128)} %broadcast_in_dim.23) | data formatting | bytes 6291456 | tf_op jit(solution)/shard_map/reshape | solution.py:33
  123.9 34.4 %all-gather.23.cloned.1.call-done = bf16[1,1024,1536]{2,1,0:T(8,128)(2,1)} async-done(((bf16[1,1024,768]{2,1,0:T(8,128)(2,1)}), bf16[1,1024,1536]{2,1,0:T(8,128)(2,1)}) %all-gather.23.cloned.1.call-update) | async-done | bytes 3145744 | tf_op jit(solution)/shard_map/all_gather | solution.py:32
  158.3 6.1 %fusion.10 = bf16[1024,768]{1,0:T(8,128)(2,1)S(1)} fusion(f32[1024,768]{1,0:T(8,128)} %reshape.39, bf16[1536,768]{1,0:T(8,128)(2,1)S(1)} %copy-done, bf16[1,1024,1536]{2,1,0:T(8,128)(2,1)} %all-gather.23.cloned.1.call-done, f32[768]{0:T(1024)S(1)} %copy-done.8, f32[768]{0:T(1024)S(1)} %copy-done.9), kind=kOutput, calls=%fused_computation.14 | convolution fusion | flops 2425356288 | bytes 10229760 | tf_op jit(solution)/shard_map/dot_general | solution.py:27
  164.4 3.4 collective-permute-start.2
  169.1 4.1 collective-permute-done.3
  173.3 7.6 %concatenate.7 = bf16[1026,768]{1,0:T(8,128)(2,1)S(1)} concatenate(bf16[1,768]{1,0:T(2,128)(2,1)S(1)} %collective-permute-done.2, bf16[1024,768]{1,0:T(8,128)(2,1)} %copy-done.2, bf16[1,768]{1,0:T(2,128)(2,1)S(1)} %collective-permute-done.3), dimensions={0} | concatenate | bytes 3151872 | tf_op jit(solution)/shard_map/concatenate | solution.py:16
  183.3 44.1 %all-gather.15.cloned.1.call-done = bf16[1024,1536]{1,0:T(8,128)(2,1)} async-done(((bf16[1024,768]{1,0:T(8,128)(2,1)}), bf16[1024,1536]{1,0:T(8,128)(2,1)}) %all-gather.15.cloned.1.call-update) | async-done | bytes 3145744 | tf_op jit(solution)/shard_map/all_gather | solution.py:40
  227.5 5.2 %convolution_convert_fusion = bf16[1024,768]{1,0:T(8,128)(2,1)S(1)} fusion(bf16[1024,1536]{1,0:T(8,128)(2,1)} %all-gather.15.cloned.1.call-done, bf16[1536,768]{1,0:T(8,128)(2,1)} %param.30), kind=kOutput, calls=%fused_computation.24 | convolution fusion | flops 2416705536 | bytes 7077888 | tf_op jit(solution)/shard_map/dot_general | solution.py:27
  232.8 3.4 collective-permute-done.4
  236.2 41.6 %all_to_all.18 = bf16[4,256,768]{2,1,0:T(8,128)(2,1)S(1)} all-to-all(bf16[4,256,768]{2,1,0:T(8,128)(2,1)S(1)} %bitcast.35), channel_id=1, replica_groups=mesh['group'=2,'context'=4,'tensor'=2,'strand'=2] {'context'}, dimensions={0} | all-to-all | bytes 3145728 | tf_op jit(solution)/shard_map/all_to_all | solution.py:96
  277.8 15.2 %all_to_all.14 = bf16[4,256,768]{2,1,0:T(8,128)(2,1)} reverse(bf16[4,256,768]{2,1,0:T(8,128)(2,1)S(1)} %all_to_all.18), dimensions={0,1} | reverse | bytes 3145728 | tf_op jit(solution)/shard_map/all_to_all | solution.py:99
  293.0 40.0 %all_to_all.19 = bf16[4,256,768]{2,1,0:T(8,128)(2,1)S(1)} all-to-all(bf16[4,256,768]{2,1,0:T(8,128)(2,1)} %all_to_all.14), channel_id=1, replica_groups=mesh['group'=2,'context'=4,'tensor'=2,'strand'=2] {'context'}, dimensions={0} | all-to-all | bytes 3145728 | tf_op jit(solution)/shard_map/all_to_all | solution.py:99
  335.1 42.5 %all-gather.19.cloned.1.call-done = bf16[1024,1536]{1,0:T(8,128)(2,1)} async-done(((bf16[1024,768]{1,0:T(8,128)(2,1)}), bf16[1024,1536]{1,0:T(8,128)(2,1)}) %all-gather.19.cloned.1.call-update) | async-done | bytes 3145744 | tf_op jit(solution)/shard_map/all_gather | solution.py:102
  377.6 14.2 %fusion.1 = bf16[1024,2048]{1,0:T(8,128)(2,1)} fusion(bf16[1024,1536]{1,0:T(8,128)(2,1)} %all-gather.19.cloned.1.call-done, bf16[1536,2048]{1,0:T(8,128)(2,1)} %param.31), kind=kOutput, calls=%fused_computation.3 | convolution fusion | flops 6457131008 | bytes 13631488 | tf_op jit(solution)/shard_map/dot_general | solution.py:27
  391.8 6.5 %copy.17 = bf16[1024,2048]{0,1:T(8,128)(2,1)} copy(bf16[1024,2048]{1,0:T(8,128)(2,1)} %fusion.1) | data formatting | bytes 8388608 | tf_op jit(solution)/shard_map/convert_element_type | solution.py:104
  398.2 7.2 %reshape.41 = bf16[1024,1024,2]{0,2,1:T(2,128)(2,1)} reshape(bf16[1024,2048]{0,1:T(8,128)(2,1)} %copy.17) | data formatting | bytes 8388608 | tf_op jit(solution)/shard_map/reshape | solution.py:46
  405.4 37.8 %rev.7 = bf16[1024,1024,2]{0,2,1:T(2,128)(2,1)} reverse(bf16[1024,1024,2]{0,2,1:T(2,128)(2,1)} %reshape.41), dimensions={2} | reverse | bytes 8388608 | tf_op jit(solution)/shard_map/rev | solution.py:46
  443.2 7.2 %reshape.42 = bf16[1024,2048]{0,1:T(8,128)(2,1)} reshape(bf16[1024,1024,2]{0,2,1:T(2,128)(2,1)} %rev.7) | data formatting | bytes 8388608 | tf_op jit(solution)/shard_map/reshape | solution.py:46
  450.5 6.5 %copy.18 = bf16[1024,2048]{1,0:T(8,128)(2,1)} copy(bf16[1024,2048]{0,1:T(8,128)(2,1)} %reshape.42) | data formatting | bytes 8388608 | tf_op jit(solution)/shard_map/reshape | solution.py:46
  457.0 17.6 %fusion.2 = bf16[1,1024,2048]{2,1,0:T(8,128)(2,1)} fusion(bf16[1024,2048]{1,0:T(8,128)(2,1)} %copy.18, bf16[1024,2048]{1,0:T(8,128)(2,1)} %fusion.1, pred[2048]{0:T(1024)(128)(4,1)S(1)} %add_compare_fusion, bf16[1024,1536]{1,0:T(8,128)(2,1)} %all-gather.17.cloned.1.call-done, bf16[1536,2048]{1,0:T(8,128)(2,1)} %param.31), kind=kOutput, calls=%fused_computation.6 | convolution fusion | flops 6469713920 | bytes 22022144 | tf_op jit(solution)/shard_map/dot_general | solution.py:27
  (53 shorter events, 12.1 us)
Async XLA Ops:
  6.5 151.7 %copy-start = (bf16[1536,768]{1,0:T(8,128)(2,1)S(1)}, bf16[1536,768]{1,0:T(8,128)(2,1)}, u32[]{:S(2)}) copy-start(bf16[1536,768]{1,0:T(8,128)(2,1)} %param.26) | copy-start | bytes 7077892
  6.5 32.3 %all-gather.21.cloned.1.call-start = ((), (), s32[]{:S(2)}) async-start(), calls=%async_computation.7 | async-start | bytes 2359296 | tf_op jit(solution)/shard_map/all_gather | solution.py:32
  7.3 72.8 %all-gather.11.cloned.1.call-start = ((), (), s32[]{:S(2)}) async-start(), calls=%async_computation.2 | async-start | bytes 2359296 | tf_op jit(solution)/shard_map/all_gather | solution.py:40
  22.8 4.9 %copy-start.4 = (bf16[3,768]{1,0:T(4,128)(2,1)S(1)}, bf16[3,768]{1,0:T(4,128)(2,1)}, u32[]{:S(2)}) copy-start(bf16[3,768]{1,0:T(4,128)(2,1)} %param.23) | copy-start | bytes 13828
  22.8 16.1 %copy-start.6 = (f32[768]{0:T(1024)S(1)}, f32[768]{0:T(1024)}, u32[]{:S(2)}) copy-start(f32[768]{0:T(1024)} %param.22) | copy-start | bytes 9220
  22.8 16.1 %copy-start.7 = (f32[768]{0:T(1024)S(1)}, f32[768]{0:T(1024)}, u32[]{:S(2)}) copy-start(f32[768]{0:T(1024)} %param.21) | copy-start | bytes 9220
  43.2 4.7 collective-permute-start
  46.6 5.5 %collective-permute-start.1 = (bf16[1,768]{1,0:T(2,128)(2,1)S(1)}, bf16[1,768]{1,0:T(2,128)(2,1)S(1)}, u32[]{:S(2)}, u32[]{:S(2)}) collective-permute-start(bf16[1,768]{1,0:T(2,128)(2,1)S(1)} %get-tuple-element.14), channel_id=1, source_target_pairs={{4,0},{8,4},{12,8},{5,1},{9,5},{13,9},{6,2},{10,6},{14,10},{7,3},{... | collective-permute-start | bytes 4616 | tf_op jit(solution)/shard_map/ppermute | solution.py:15
  53.7 58.2 %all-gather.13.cloned.1.call-start = ((), (), s32[]{:S(2)}) async-start(), calls=%async_computation.3 | async-start | bytes 2359296 | tf_op jit(solution)/shard_map/all_gather | solution.py:31
  84.5 0.8 copy-start.5
  84.5 73.7 %all-gather.23.cloned.1.call-start = ((), (), s32[]{:S(2)}) async-start(), calls=%async_computation.8 | async-start | bytes 4718592 | tf_op jit(solution)/shard_map/all_gather | solution.py:32
  85.1 142.3 %all-gather.15.cloned.1.call-start = ((), (), s32[]{:S(2)}) async-start(), calls=%async_computation.4 | async-start | bytes 4718592 | tf_op jit(solution)/shard_map/all_gather | solution.py:40
  118.2 40.1 %copy-start.8 = (f32[768]{0:T(1024)S(1)}, f32[768]{0:T(1024)}, u32[]{:S(2)}) copy-start(f32[768]{0:T(1024)} %param.28) | copy-start | bytes 9220
  118.2 40.1 %copy-start.9 = (f32[768]{0:T(1024)S(1)}, f32[768]{0:T(1024)}, u32[]{:S(2)}) copy-start(f32[768]{0:T(1024)} %param.27) | copy-start | bytes 9220
  164.4 4.8 copy-start.2
  164.4 4.7 collective-permute-start.2
  167.8 5.5 %collective-permute-start.3 = (bf16[1,768]{1,0:T(2,128)(2,1)S(1)}, bf16[1,768]{1,0:T(2,128)(2,1)S(1)}, u32[]{:S(2)}, u32[]{:S(2)}) collective-permute-start(bf16[1,768]{1,0:T(2,128)(2,1)S(1)} %get-tuple-element.11), channel_id=1, source_target_pairs={{4,0},{8,4},{12,8},{5,1},{9,5},{13,9},{6,2},{10,6},{14,10},{7,3},{... | collective-permute-start | bytes 4616 | tf_op jit(solution)/shard_map/ppermute | solution.py:15
  183.3 194.3 %all-gather.19.cloned.1.call-start = ((), (), s32[]{:S(2)}) async-start(), calls=%async_computation.6 | async-start | bytes 4718592 | tf_op jit(solution)/shard_map/all_gather | solution.py:102
  232.7 3.5 copy-start.3
  232.7 3.5 collective-permute-start.4
  334.3 122.7 %all-gather.17.cloned.1.call-start = ((), (), s32[]{:S(2)}) async-start(), calls=%async_computation.5 | async-start | bytes 4718592 | tf_op jit(solution)/shard_map/all_gather | solution.py:101
  457.0 17.6 %copy-start.1 = (bf16[1536,768]{1,0:T(8,128)(2,1)S(1)}, bf16[1536,768]{1,0:T(8,128)(2,1)}, u32[]{:S(2)}) copy-start(bf16[1536,768]{1,0:T(8,128)(2,1)} %param.26) | copy-start | bytes 7077892
Sparse Core Ops, SparseCore 0:
  8.9 29.8 all-gather.20
  53.8 26.2 all-gather.10
  84.7 27.2 all-gather.12
  113.3 44.9 all-gather.22
  183.4 44.0 all-gather.14
  334.5 43.0 all-gather.18
  379.1 44.9 all-gather.16
where the time goes:
time: 485 us; the launch traced here: 481 us
  waiting for transfers between devices  199 us (41%)
  local copies, waits for them, and re-layouts  103 us (21%)
  blocking collectives  94.7 us (20%)
  matrix products  57.8 us (12%)
  between operations  13.7 us (3%)
  starting transfers between devices  10.1 us (2%)
    all_gather x2, waiting for transfers between devices, upsample_section(): lax.all_gather(depthwise, 'tensor', axis=1, tiled=True)  70.5 us
    dot_general x8, matrix products, contract(): return jnp.dot(portion, weight, preferred_element_type=jnp.float32)  57.8 us
    all_gather x2, waiting for transfers between devices, upsample_section(): lax.all_gather(lateral_in, 'tensor', axis=1, tiled=True)  45.6 us
    all_gather x1, waiting for transfers between devices, on_device(): lax.all_gather(partner, 'tensor', axis=1, tiled=True)  42.5 us
    all_to_all x1, blocking collectives, on_device(): lax.all_to_all(crossed, 'context', split_axis=0, concat_axis=0, tiled=True)  41.6 us
    all_to_all x1, blocking collectives, on_device(): lax.all_to_all(reordered, 'context', split_axis=0, concat_axis=0, tiled=T...  40 us
    rev x1, local copies, waits for them, and re-layouts, flip_tracks(): values.reshape(row_count, track_count // 2, 2)[:, :, ::-1]  37.8 us
    all_gather x1, waiting for transfers between devices, upsample_section(): lax.all_gather(coarse, 'tensor', axis=1, tiled=True)  26.5 us
  transfers between devices with their start and end apart: 12, of which 9 were waited for; matrix products, arithmetic and copies ran while one was open for 21% of the time, Pallas kernels for 0%

commit v1 on v0

--- a/solution.py
+++ b/solution.py
@@ -41,13 +41,20 @@
     return mixed_out.astype(jnp.bfloat16)
 
 
-def flip_tracks(values, total_tracks):
-    row_count, track_count = values.shape
-    swapped = values.reshape(row_count, track_count // 2, 2)[:, :, ::-1].reshape(
-        row_count, track_count
-    )
+def flip_weight(weight, total_tracks):
+    depth, track_count = weight.shape
+    tile = 128
+    row = lax.broadcasted_iota(jnp.int32, (tile, tile), 0)
+    column = lax.broadcasted_iota(jnp.int32, (tile, tile), 1)
+    swap = (row == (column ^ 1)).astype(weight.dtype)
+    swapped = jnp.einsum(
+        "kbi,ij->kbj",
+        weight.reshape(depth, track_count // tile, tile),
+        swap,
+        preferred_element_type=weight.dtype,
+    ).reshape(depth, track_count)
     track_index = lax.axis_index("tensor") * track_count + jnp.arange(track_count)
-    return jnp.where((track_index < total_tracks // 2)[None, :], swapped, values)
+    return jnp.where((track_index < total_tracks // 2)[None, :], swapped, weight)
 
 
 def on_device(
@@ -89,19 +96,24 @@
         mixing_fine,
     )
     total_tracks = head_weight.shape[1] * lax.axis_size("tensor")
-    slab_count = lax.axis_size("context")
     row_count, width = hidden_fine.shape
-    block_rows = row_count // slab_count
-    crossed = from_partner(hidden_fine, "strand", 0)
-    spread_rows = lax.all_to_all(crossed, "context", split_axis=0, concat_axis=0, tiled=True)
-    blocks = spread_rows.reshape(slab_count, block_rows, width)
-    reordered = jnp.flip(blocks, (0, 1)).reshape(row_count, width)
-    returned = lax.all_to_all(reordered, "context", split_axis=0, concat_axis=0, tiled=True)
-    partner = jnp.flip(returned.reshape(slab_count, block_rows, width), 0).reshape(row_count, width)
+    slabs, strands = lax.axis_size("context"), lax.axis_size("strand")
+    count = slabs * strands
+    crossed = lax.ppermute(
+        hidden_fine, ("context", "strand"), [(i, count - 1 - i) for i in range(count)]
+    )
     own_logits = contract(lax.all_gather(hidden_fine, "tensor", axis=1, tiled=True), head_weight)
-    partner_logits = contract(lax.all_gather(partner, "tensor", axis=1, tiled=True), head_weight)
     predicted = jax.nn.softplus(own_logits).astype(jnp.bfloat16)
-    mirrored = flip_tracks(jax.nn.softplus(partner_logits).astype(jnp.bfloat16), total_tracks)
+    reverse = jnp.eye(256, dtype=jnp.bfloat16)[::-1]
+    blocks = crossed.reshape(row_count // 256, 256, width)[::-1]
+    partner = jnp.einsum(
+        "ij,bjk->bik", reverse, blocks, preferred_element_type=jnp.bfloat16
+    ).reshape(row_count, width)
+    flipped_head = flip_weight(head_weight, total_tracks)
+    partner_logits = contract(
+        lax.all_gather(partner, "tensor", axis=1, tiled=True), flipped_head
+    )
+    mirrored = jax.nn.softplus(partner_logits).astype(jnp.bfloat16)
     averaged = (0.5 * (predicted.astype(jnp.float32) + mirrored.astype(jnp.float32))).astype(
         jnp.bfloat16
     )

time: 485 us -> 380 us (0.78)
  blocking collectives: 94.7 us -> 13 us
  local copies, waits for them, and re-layouts: 103 us -> 29.8 us
  waiting for transfers between devices: 199 us -> 236 us
  matrix products: 57.8 us -> 70.1 us
    all_to_all x2 -> x0, blocking collectives: 81.7 us -> none  [the longest x1 41.6 us: on_device(): lax.all_to_all(crossed, 'context', split_axis=0, concat_axis=0, tiled=True)]
    rev x1, local copies, waits for them, and re-layouts: 37.8 us -> 0.18 us  [on_device(): reverse = jnp.eye(256, dtype=jnp.bfloat16)[::-1]]
    ppermute x1, waiting for transfers between devices: 3.4 us -> 35.7 us  [on_device(): lax.ppermute(hidden_fine, ('context', 'strand'), [(i, count - 1 - i) for...]
    all_to_all x1 -> x0, local copies, waits for them, and re-layouts: 15.2 us -> none  [on_device(): lax.all_to_all(reordered, 'context', split_axis=0, concat_axis=0, tiled=T...]
    reshape x3 -> x1, local copies, waits for them, and re-layouts: 20.9 us -> 8.7 us  [flip_weight(): swapped = jnp.einsum('kbi,ij->kbj', weight.reshape(depth, track_count //...]
    dot_general x0 -> x2, matrix products: none -> 9.12 us  [the longest x1 7.34 us: flip_weight(): jnp.einsum('kbi,ij->kbj', weight.reshape(depth, track_count // tile, tile...]
    convert_element_type x1 -> x0, local copies, waits for them, and re-layouts: 6.45 us -> none  [on_device(): jax.nn.softplus(partner_logits).astype(jnp.bfloat16)]
    all_gather x1, waiting for transfers between devices: 42.5 us -> 48.3 us  [on_device(): lax.all_gather(partner, 'tensor', axis=1, tiled=True)]
  transfers between devices with their start and end apart: 12 -> 12, of which waited for: 9 -> 9; matrix products, arithmetic and copies ran while one was open for 21% -> 13% of each run, Pallas kernels for 0% -> 0%
where the time goes in v1:
time: 380 us
  waiting for transfers between devices  236 us (62%)
  matrix products  70.1 us (18%)
  local copies, waits for them, and re-layouts  29.8 us (8%)
  between operations  13.7 us (4%)
  blocking collectives  13 us (3%)
  starting transfers between devices  12.9 us (3%)
  other arithmetic  3.96 us (1%)
    all_gather x2, waiting for transfers between devices, upsample_section(): lax.all_gather(depthwise, 'tensor', axis=1, tiled=True)  70.5 us
    dot_general x8, matrix products, contract(): return jnp.dot(portion, weight, preferred_element_type=jnp.float32)  61 us
    all_gather x1, waiting for transfers between devices, on_device(): lax.all_gather(partner, 'tensor', axis=1, tiled=True)  48.3 us
    all_gather x2, waiting for transfers between devices, upsample_section(): lax.all_gather(lateral_in, 'tensor', axis=1, tiled=True)  45.6 us
    ppermute x1, waiting for transfers between devices, on_device(): lax.ppermute(hidden_fine, ('context', 'strand'), [(i, count - 1 - i) for...  35.7 us
    all_gather x1, waiting for transfers between devices, upsample_section(): lax.all_gather(coarse, 'tensor', axis=1, tiled=True)  26.5 us
    all_gather x1, blocking collectives, upsample_section(): lax.all_gather(coarse, 'tensor', axis=1, tiled=True)  13 us
    reshape x2, local copies, waits for them, and re-layouts, upsample_section(): upsampled = jnp.repeat(lifted, 2, axis=0)  8.81 us
  transfers between devices with their start and end apart: 12, of which 9 were waited for; matrix products, arithmetic and copies ran while one was open for 13% of the time, Pallas kernels for 0%

profile of v1, /device:TPU:0, one launch (start us, length us, event | category | flops | bytes accessed | tf_op | source)
XLA Modules:
  0.0 379.7 jit_solution(933061893078118044)
XLA Ops:
  7.3 13.0 %all-gather = bf16[1,256,1536]{2,1,0:T(8,128)(2,1)S(1)} all-gather(bf16[1,256,768]{2,1,0:T(8,128)(2,1)} %param.16), channel_id=2, replica_groups=mesh['group'=2,'context'=4,'tensor'=2,'strand'=2] {'tensor'}, dimensions={2}, use_global_device_ids=true | all-gather | bytes 1179648 | tf_op jit(solution)/shard_map/all_gather | solution.py:31
  20.3 2.5 fusion.41
  22.8 1.7 broadcast_in_dim.22
  24.5 3.1 reshape.27
  27.6 11.2 %all-gather.21.cloned.1.call-done = bf16[1,512,1536]{2,1,0:T(8,128)(2,1)} async-done(((bf16[1,512,768]{2,1,0:T(8,128)(2,1)}), bf16[1,512,1536]{2,1,0:T(8,128)(2,1)}) %all-gather.21.cloned.1.call-update) | async-done | bytes 1572880 | tf_op jit(solution)/shard_map/all_gather | solution.py:32
  38.8 4.3 %fusion.33 = bf16[512,768]{1,0:T(8,128)(2,1)S(1)} fusion(f32[512,768]{1,0:T(8,128)} %reshape.27, bf16[1536,768]{1,0:T(8,128)(2,1)} %param.20, bf16[1,512,1536]{2,1,0:T(8,128)(2,1)} %all-gather.21.cloned.1.call-done, f32[768]{0:T(1024)S(1)} %copy-done.5, f32[768]{0:T(1024)S(1)} %copy-done.6), kind=kOutput, calls=%fused_computation.38 | convolution fusion | flops 1212678144 | bytes 6297600 | tf_op jit(solution)/shard_map/dot_general | solution.py:27
  43.2 3.4 collective-permute-start
  46.6 1.3 collective-permute-start.1
  47.9 4.1 %collective-permute-done.1 = bf16[1,768]{1,0:T(2,128)(2,1)S(1)} collective-permute-done((bf16[1,768]{1,0:T(2,128)(2,1)S(1)}, bf16[1,768]{1,0:T(2,128)(2,1)S(1)}, u32[]{:S(2)}, u32[]{:S(2)}) %collective-permute-start.1) | collective-permute-done | bytes 1568 | tf_op jit(solution)/shard_map/ppermute | solution.py:15
  52.3 1.4 fusion.35
  53.7 26.4 %all-gather.11.cloned.1.call-done = bf16[512,1536]{1,0:T(8,128)(2,1)} async-done(((bf16[512,768]{1,0:T(8,128)(2,1)}), bf16[512,1536]{1,0:T(8,128)(2,1)}) %all-gather.11.cloned.1.call-update) | async-done | bytes 1572880 | tf_op jit(solution)/shard_map/all_gather | solution.py:40
  80.1 4.4 %convolution_convert_fusion.1 = bf16[512,768]{1,0:T(8,128)(2,1)} fusion(bf16[512,1536]{1,0:T(8,128)(2,1)} %all-gather.11.cloned.1.call-done, bf16[1536,768]{1,0:T(8,128)(2,1)} %param.24), kind=kOutput, calls=%fused_computation.47 | convolution fusion | flops 1208352768 | bytes 4718592 | tf_op jit(solution)/shard_map/dot_general | solution.py:27
  85.4 26.5 %all-gather.13.cloned.1.call-done = bf16[512,1536]{1,0:T(8,128)(2,1)} async-done(((bf16[512,768]{1,0:T(8,128)(2,1)}), bf16[512,1536]{1,0:T(8,128)(2,1)}) %all-gather.13.cloned.1.call-update) | async-done | bytes 1572880 | tf_op jit(solution)/shard_map/all_gather | solution.py:31
  111.9 3.5 fusion.51
  115.4 2.7 broadcast_in_dim.23
  118.2 5.7 %reshape.28 = f32[1024,768]{1,0:T(8,128)} reshape(f32[512,2,768]{2,1,0:T(2,128)} %broadcast_in_dim.23) | data formatting | bytes 6291456 | tf_op jit(solution)/shard_map/reshape | solution.py:33
  123.8 34.4 %all-gather.23.cloned.1.call-done = bf16[1,1024,1536]{2,1,0:T(8,128)(2,1)} async-done(((bf16[1,1024,768]{2,1,0:T(8,128)(2,1)}), bf16[1,1024,1536]{2,1,0:T(8,128)(2,1)}) %all-gather.23.cloned.1.call-update) | async-done | bytes 3145744 | tf_op jit(solution)/shard_map/all_gather | solution.py:32
  158.3 6.1 %fusion.18 = bf16[1024,768]{1,0:T(8,128)(2,1)S(1)} fusion(f32[1024,768]{1,0:T(8,128)} %reshape.28, bf16[1536,768]{1,0:T(8,128)(2,1)S(1)} %copy-done, bf16[1,1024,1536]{2,1,0:T(8,128)(2,1)} %all-gather.23.cloned.1.call-done, f32[768]{0:T(1024)S(1)} %copy-done.7, f32[768]{0:T(1024)S(1)} %copy-done.8), kind=kOutput, calls=%fused_computation.20 | convolution fusion | flops 2425356288 | bytes 10229760 | tf_op jit(solution)/shard_map/dot_general | solution.py:27
  164.4 3.4 collective-permute-start.2
  169.1 4.1 %collective-permute-done.3 = bf16[1,768]{1,0:T(2,128)(2,1)S(1)} collective-permute-done((bf16[1,768]{1,0:T(2,128)(2,1)S(1)}, bf16[1,768]{1,0:T(2,128)(2,1)S(1)}, u32[]{:S(2)}, u32[]{:S(2)}) %collective-permute-start.3) | collective-permute-done | bytes 1568 | tf_op jit(solution)/shard_map/ppermute | solution.py:15
  173.3 7.6 %concatenate.7 = bf16[1026,768]{1,0:T(8,128)(2,1)S(1)} concatenate(bf16[1,768]{1,0:T(2,128)(2,1)S(1)} %collective-permute-done.2, bf16[1024,768]{1,0:T(8,128)(2,1)} %copy-done.2, bf16[1,768]{1,0:T(2,128)(2,1)S(1)} %collective-permute-done.3), dimensions={0} | concatenate | bytes 3151872 | tf_op jit(solution)/shard_map/concatenate | solution.py:16
  181.1 2.1 fusion.20
  183.3 44.1 %all-gather.15.cloned.1.call-done = bf16[1024,1536]{1,0:T(8,128)(2,1)} async-done(((bf16[1024,768]{1,0:T(8,128)(2,1)}), bf16[1024,1536]{1,0:T(8,128)(2,1)}) %all-gather.15.cloned.1.call-update) | async-done | bytes 3145744 | tf_op jit(solution)/shard_map/all_gather | solution.py:40
  227.4 6.4 %convolution_convert_fusion = bf16[1024,768]{1,0:T(8,128)(2,1)} fusion(bf16[1024,1536]{1,0:T(8,128)(2,1)} %all-gather.15.cloned.1.call-done, bf16[1536,768]{1,0:T(8,128)(2,1)} %param.30), kind=kOutput, calls=%fused_computation.30 | convolution fusion | flops 2416705536 | bytes 7077888 | tf_op jit(solution)/shard_map/dot_general | solution.py:27
  234.1 2.8 collective-permute-start.4
  237.2 35.7 %collective-permute-done.4 = bf16[1024,768]{1,0:T(8,128)(2,1)S(1)} collective-permute-done((bf16[1024,768]{1,0:T(8,128)(2,1)}, bf16[1024,768]{1,0:T(8,128)(2,1)S(1)}, u32[]{:S(2)}, u32[]{:S(2)}) %collective-permute-start.4) | collective-permute-done | bytes 1572896 | tf_op jit(solution)/shard_map/ppermute | solution.py:102
  272.9 1.8 fusion.44
  274.7 7.3 %fusion.2 = bf16[128,1536,16]{1,0,2:T(8,128)(2,1)} fusion(s32[128]{0:T(128)S(1)} %iota_xor_fusion, bf16[1536,2048]{1,0:T(8,128)(2,1)} %param.31), kind=kOutput, calls=%fused_computation.5 | convolution fusion | flops 805322752 | bytes 12583424 | tf_op jit(solution)/shard_map/kbi,ij->kbj/dot_general | solution.py:50
  282.0 8.7 %copy.18 = bf16[1536,2048]{1,0:T(8,128)(2,1)} copy(bf16[1536,2048]{0,1:T(8,128)(2,1)} %bitcast.48) | data formatting | bytes 12582912 | tf_op jit(solution)/shard_map/reshape | solution.py:55
  290.8 11.7 %fusion.52 = f32[1024,2048]{1,0:T(8,128)} fusion(bf16[1024,1536]{1,0:T(8,128)(2,1)} %all-gather.17.cloned.1.call-done, bf16[1536,2048]{1,0:T(8,128)(2,1)} %param.31), kind=kOutput, calls=%fused_computation.69 | convolution fusion | flops 6442450944 | bytes 17825792 | tf_op jit(solution)/shard_map/dot_general | solution.py:27
  302.4 48.3 %all-gather.19.cloned.1.call-done = bf16[1024,1536]{1,0:T(8,128)(2,1)} async-done(((bf16[1024,768]{1,0:T(8,128)(2,1)}), bf16[1024,1536]{1,0:T(8,128)(2,1)}) %all-gather.19.cloned.1.call-update) | async-done | bytes 3145744 | tf_op jit(solution)/shard_map/all_gather | solution.py:114
  350.7 22.1 %fusion.8 = bf16[1,1024,2048]{2,1,0:T(8,128)(2,1)} fusion(f32[1024,2048]{1,0:T(8,128)} %fusion.52, bf16[1024,1536]{1,0:T(8,128)(2,1)} %all-gather.19.cloned.1.call-done, bf16[1536,2048]{1,0:T(8,128)(2,1)} %copy.18, bf16[1536,2048]{1,0:T(8,128)(2,1)} %param.31, pred[2048]{0:T(1024)(128)(4,1)S(1)} %add_compare_fusion), kind=kOutput, calls=%fused_computation.12 | convolution fusion | flops 6485442560 | bytes 28313600 | tf_op jit(solution)/shard_map/dot_general | solution.py:27
  (48 shorter events, 4.0 us)
Async XLA Ops:
  6.5 151.7 %copy-start = (bf16[1536,768]{1,0:T(8,128)(2,1)S(1)}, bf16[1536,768]{1,0:T(8,128)(2,1)}, u32[]{:S(2)}) copy-start(bf16[1536,768]{1,0:T(8,128)(2,1)} %param.26) | copy-start | bytes 7077892
  6.5 32.3 %all-gather.21.cloned.1.call-start = ((), (), s32[]{:S(2)}) async-start(), calls=%async_computation.5 | async-start | bytes 2359296 | tf_op jit(solution)/shard_map/all_gather | solution.py:32
  7.3 72.8 %all-gather.11.cloned.1.call-start = ((), (), s32[]{:S(2)}) async-start(), calls=%async_computation | async-start | bytes 2359296 | tf_op jit(solution)/shard_map/all_gather | solution.py:40
  22.8 4.9 %copy-start.3 = (bf16[3,768]{1,0:T(4,128)(2,1)S(1)}, bf16[3,768]{1,0:T(4,128)(2,1)}, u32[]{:S(2)}) copy-start(bf16[3,768]{1,0:T(4,128)(2,1)} %param.23) | copy-start | bytes 13828
  22.8 16.1 %copy-start.5 = (f32[768]{0:T(1024)S(1)}, f32[768]{0:T(1024)}, u32[]{:S(2)}) copy-start(f32[768]{0:T(1024)} %param.22) | copy-start | bytes 9220
  22.8 16.1 %copy-start.6 = (f32[768]{0:T(1024)S(1)}, f32[768]{0:T(1024)}, u32[]{:S(2)}) copy-start(f32[768]{0:T(1024)} %param.21) | copy-start | bytes 9220
  43.2 4.7 %collective-permute-start = (bf16[1,768]{1,0:T(2,128)(2,1)S(1)}, bf16[1,768]{1,0:T(2,128)(2,1)S(1)}, u32[]{:S(2)}, u32[]{:S(2)}) collective-permute-start(bf16[1,768]{1,0:T(2,128)(2,1)S(1)} %get-tuple-element.13), channel_id=1, source_target_pairs={{0,4},{4,8},{8,12},{1,5},{5,9},{9,13},{2,6},{6,10},{10,14},{3,7},{... | collective-permute-start | bytes 4616 | tf_op jit(solution)/shard_map/ppermute | solution.py:12
  46.6 5.5 %collective-permute-start.1 = (bf16[1,768]{1,0:T(2,128)(2,1)S(1)}, bf16[1,768]{1,0:T(2,128)(2,1)S(1)}, u32[]{:S(2)}, u32[]{:S(2)}) collective-permute-start(bf16[1,768]{1,0:T(2,128)(2,1)S(1)} %get-tuple-element.14), channel_id=1, source_target_pairs={{4,0},{8,4},{12,8},{5,1},{9,5},{13,9},{6,2},{10,6},{14,10},{7,3},{... | collective-permute-start | bytes 4616 | tf_op jit(solution)/shard_map/ppermute | solution.py:15
  53.7 31.7 %copy-start.4 = (bf16[3,768]{1,0:T(4,128)(2,1)S(1)}, bf16[3,768]{1,0:T(4,128)(2,1)}, u32[]{:S(2)}) copy-start(bf16[3,768]{1,0:T(4,128)(2,1)} %param.29) | copy-start | bytes 13828
  53.7 58.2 %all-gather.13.cloned.1.call-start = ((), (), s32[]{:S(2)}) async-start(), calls=%async_computation.1 | async-start | bytes 2359296 | tf_op jit(solution)/shard_map/all_gather | solution.py:31
  84.5 73.7 %all-gather.23.cloned.1.call-start = ((), (), s32[]{:S(2)}) async-start(), calls=%async_computation.6 | async-start | bytes 4718592 | tf_op jit(solution)/shard_map/all_gather | solution.py:32
  85.1 142.3 %all-gather.15.cloned.1.call-start = ((), (), s32[]{:S(2)}) async-start(), calls=%async_computation.2 | async-start | bytes 4718592 | tf_op jit(solution)/shard_map/all_gather | solution.py:40
  118.2 40.1 %copy-start.7 = (f32[768]{0:T(1024)S(1)}, f32[768]{0:T(1024)}, u32[]{:S(2)}) copy-start(f32[768]{0:T(1024)} %param.28) | copy-start | bytes 9220
  118.2 40.1 %copy-start.8 = (f32[768]{0:T(1024)S(1)}, f32[768]{0:T(1024)}, u32[]{:S(2)}) copy-start(f32[768]{0:T(1024)} %param.27) | copy-start | bytes 9220
  164.4 4.8 %copy-start.2 = (bf16[1024,768]{1,0:T(8,128)(2,1)}, bf16[1024,768]{1,0:T(8,128)(2,1)S(1)}, u32[]{:S(2)}) copy-start(bf16[1024,768]{1,0:T(8,128)(2,1)S(1)} %fusion.18) | copy-start | bytes 4718596
  164.4 4.7 %collective-permute-start.2 = (bf16[1,768]{1,0:T(2,128)(2,1)S(1)}, bf16[1,768]{1,0:T(2,128)(2,1)S(1)}, u32[]{:S(2)}, u32[]{:S(2)}) collective-permute-start(bf16[1,768]{1,0:T(2,128)(2,1)S(1)} %get-tuple-element.12), channel_id=1, source_target_pairs={{0,4},{4,8},{8,12},{1,5},{5,9},{9,13},{2,6},{6,10},{10,14},{3,7},{... | collective-permute-start | bytes 4616 | tf_op jit(solution)/shard_map/ppermute | solution.py:12
  167.8 5.5 %collective-permute-start.3 = (bf16[1,768]{1,0:T(2,128)(2,1)S(1)}, bf16[1,768]{1,0:T(2,128)(2,1)S(1)}, u32[]{:S(2)}, u32[]{:S(2)}) collective-permute-start(bf16[1,768]{1,0:T(2,128)(2,1)S(1)} %get-tuple-element.11), channel_id=1, source_target_pairs={{4,0},{8,4},{12,8},{5,1},{9,5},{13,9},{6,2},{10,6},{14,10},{7,3},{... | collective-permute-start | bytes 4616 | tf_op jit(solution)/shard_map/ppermute | solution.py:15
  183.3 107.5 %all-gather.17.cloned.1.call-start = ((), (), s32[]{:S(2)}) async-start(), calls=%async_computation.3 | async-start | bytes 4718592 | tf_op jit(solution)/shard_map/all_gather | solution.py:105
  233.8 116.9 %all-gather.19.cloned.1.call-start = ((), (), s32[]{:S(2)}) async-start(), calls=%async_computation.4 | async-start | bytes 4718592 | tf_op jit(solution)/shard_map/all_gather | solution.py:114
  234.1 38.8 %collective-permute-start.4 = (bf16[1024,768]{1,0:T(8,128)(2,1)}, bf16[1024,768]{1,0:T(8,128)(2,1)S(1)}, u32[]{:S(2)}, u32[]{:S(2)}) collective-permute-start(bf16[1024,768]{1,0:T(8,128)(2,1)} %convolution_convert_fusion), channel_id=1, source_target_pairs={{0,13},{1,12},{4,9},{5,8},{8,5},{9,4},{12,1},{13,0},{2,15},{3,14},... | collective-permute-start | bytes 4718600 | tf_op jit(solution)/shard_map/ppermute | solution.py:102
  350.7 22.1 %copy-start.1 = (bf16[1536,768]{1,0:T(8,128)(2,1)S(1)}, bf16[1536,768]{1,0:T(8,128)(2,1)}, u32[]{:S(2)}) copy-start(bf16[1536,768]{1,0:T(8,128)(2,1)} %param.26) | copy-start | bytes 7077892
Sparse Core Ops, SparseCore 0:
  8.9 29.8 all-gather.20
  53.8 26.2 all-gather.10
  84.7 27.2 all-gather.12
  113.3 44.9 all-gather.22
  183.4 44.0 all-gather.14
  234.0 44.9 all-gather.16
  280.5 70.2 all-gather.18

commit v2 on v0

v2 whole, which is shorter than its diff:
```python
import jax
import jax.numpy as jnp
from jax import lax
from jax.experimental import pallas as pl
from jax.experimental.pallas import tpu as pltpu
from jax.sharding import PartitionSpec as P

MESH = pl.DeviceIdType.MESH
EDGE = 16


def dot(left, right):
    return jnp.dot(left, right, preferred_element_type=jnp.float32)


def gelu(x):
    return 0.5 * x * (1.0 + jnp.tanh(0.7978845608028654 * (x + 0.044715 * (x * x * x))))


def mean_softplus(a, b):
    ea = jnp.exp(-jnp.abs(a))
    eb = jnp.exp(-jnp.abs(b))
    u = ea + eb + ea * eb
    log = jnp.where(u < 1e-3, u * (1.0 - 0.5 * u), jnp.log(1.0 + u))
    return 0.5 * (jnp.maximum(a, 0.0) + jnp.maximum(b, 0.0) + log)


class Gather:
    def __init__(self, peers, buffer, tile, send, recv):
        self.me, self.count = peers
        self.buffer, self.tile, self.send_sem, self.recv_sem = buffer, tile, send, recv
        self.tiles = buffer.shape[1] // tile

    def rows(self, i):
        return pl.ds(pl.multiple_of(i * self.tile, EDGE), self.tile)

    def copy(self, d, slot, i, source=None):
        target = self.buffer.at[slot, self.rows(i)]
        return pltpu.make_async_remote_copy(
            src_ref=target if source is None else source.at[0, self.rows(i)],
            dst_ref=target,
            send_sem=self.send_sem.at[d - 1, i],
            recv_sem=self.recv_sem.at[d - 1, i],
            device_id={"tensor": lax.rem(self.me + d, self.count)},
            device_id_type=MESH,
        )

    def start(self, i, source=None):
        for d in range(1, self.count):
            self.copy(d, self.me, i, source).start()

    def arrived(self, i):
        for d in range(1, self.count):
            self.copy(d, lax.rem(self.me + self.count - d, self.count), i).wait_recv()

    def sent(self):
        @pl.loop(0, self.tiles)
        def _(i):
            for d in range(1, self.count):
                self.copy(d, self.me, i).wait_send()


def kernel(
    sizes,
    trunk, skip_mid, skip_fine,
    coarse_mid, lateral_mid, mixing_mid, coarse_fine, lateral_fine, mixing_fine, head,
    gain_mid, shift_mid, depth_mid, gain_fine, shift_fine, depth_fine,
    out,
    trunk_all, skip_mid_all, skip_fine_all, taps_mid_all, hidden_mid_all, taps_fine_all, own_all,
    partner_all,
    active_mid, active_fine,
    w_coarse_mid, w_lateral_mid, w_mixing_mid, w_coarse_fine, w_lateral_fine, w_mixing_fine,
    w_head, w_flipped,
    expanded, turned, result, doubler, reverser, swapper,
    local_sem, out_sem,
    s0, r0, s1, r1, s2, r2, s3, r3, s4, r4, s5, r5, s6, r6, s7, r7,
    mirror_send, mirror_recv, edge_send, edge_recv,
):
    tensors, contexts, tile_mid, tile_fine = sizes
    me = lax.axis_index("tensor")
    slab = lax.axis_index("context")
    strand = lax.axis_index("strand")
    after = {"context": lax.rem(slab + 1, contexts)}
    before = {"context": lax.rem(slab + contexts - 1, contexts)}
    mirror = {"context": contexts - 1 - slab, "strand": 1 - strand}
    width = active_mid.shape[1]
    tracks = w_head.shape[1]
    step = 256 if width % 256 == 0 else width
    peers = (me, tensors)

    locals_ = []
    for source, target in (
        (trunk.at[0], trunk_all.at[me]),
        (skip_mid.at[0], skip_mid_all.at[me]),
        (head, w_head),
        (coarse_mid, w_coarse_mid),
        (lateral_mid, w_lateral_mid),
        (mixing_mid, w_mixing_mid),
        (skip_fine.at[0], skip_fine_all.at[me]),
        (coarse_fine, w_coarse_fine),
        (lateral_fine, w_lateral_fine),
        (mixing_fine, w_mixing_fine),
    ):
        copy = pltpu.make_async_copy(source, target, local_sem.at[len(locals_)])
        copy.start()
        locals_.append(copy)

    barrier = pltpu.get_barrier_semaphore()
    for d in range(1, tensors):
        pl.semaphore_signal(
            barrier, inc=1, device_id={"tensor": lax.rem(me + d, tensors)}, device_id_type=MESH
        )
    for target in (after, before, mirror):
        pl.semaphore_signal(barrier, inc=1, device_id=target, device_id_type=MESH)
    pl.semaphore_wait(barrier, tensors + 2)

    g_trunk = Gather(peers, trunk_all, trunk_all.shape[1], s0, r0)
    g_skip_mid = Gather(peers, skip_mid_all, skip_mid_all.shape[1], s1, r1)
    g_skip_fine = Gather(peers, skip_fine_all, tile_fine, s2, r2)
    g_taps_mid = Gather(peers, taps_mid_all, tile_mid, s3, r3)
    g_hidden_mid = Gather(peers, hidden_mid_all, tile_mid, s4, r4)
    g_taps_fine = Gather(peers, taps_fine_all, tile_fine, s5, r5)
    g_own = Gather(peers, own_all, tile_fine, s6, r6)
    g_partner = Gather(peers, partner_all, tile_fine, s7, r7)
    fine_tiles = g_own.tiles

    g_trunk.start(0, trunk)
    g_skip_mid.start(0, skip_mid)

    def iotas(shape):
        return (
            lax.broadcasted_iota(jnp.int32, shape, 0),
            lax.broadcasted_iota(jnp.int32, shape, 1),
        )

    row, column = iotas(doubler.shape)
    doubler[...] = jnp.where(
        (row == 2 * column) | (row == 2 * column + 1), 1.0, 0.0
    ).astype(jnp.bfloat16)
    row, column = iotas(reverser.shape)
    reverser[...] = jnp.where(row + column == tile_fine - 1, 1.0, 0.0).astype(jnp.bfloat16)
    row, column = iotas(swapper.shape)
    neighbour = jnp.where(lax.rem(column, 2) == 0, column + 1, column - 1)

    locals_[2].wait()

    @pl.loop(0, tracks // 256)
    def _(n):
        columns = pl.ds(pl.multiple_of(n * 256, 256), 256)
        first = me * tracks + n * 256
        flips = first < (tracks * tensors) // 2
        swapper[...] = jnp.where(
            row == jnp.where(flips, neighbour, column), 1.0, 0.0
        ).astype(jnp.bfloat16)
        for j in range(tensors):
            depth = pl.ds(j * width, width)
            w_flipped[depth, columns] = dot(w_head[depth, columns], swapper[...]).astype(
                jnp.bfloat16
            )

    def project(i, tile, coarse, lateral, w_coarse, w_lateral, gain, shift, active):
        half = pl.ds(pl.multiple_of(i * (tile // 2), EDGE), tile // 2)
        rows = pl.ds(pl.multiple_of(i * tile, EDGE), tile)
        for j in range(tensors):
            expanded[j, :tile] = dot(doubler[:tile, : tile // 2], coarse[j, half]).astype(
                jnp.bfloat16
            )

        @pl.loop(0, width // step)
        def _(n):
            columns = pl.ds(pl.multiple_of(n * step, 128), step)
            total = jnp.zeros((tile, step), jnp.float32)
            for j in range(tensors):
                depth = pl.ds(j * width, width)
                total += dot(expanded[j, :tile], w_coarse[depth, columns])
                total += dot(lateral[j, rows], w_lateral[depth, columns])
            value = gelu(gain[:, columns] * total + shift[:, columns])
            active[pl.ds(pl.multiple_of(EDGE + i * tile, EDGE), tile), columns] = value.astype(
                jnp.bfloat16
            )

    def edges(active, k):
        length = active.shape[0] - 2 * EDGE
        up = pltpu.make_async_remote_copy(
            src_ref=active.at[pl.ds(length, EDGE)],
            dst_ref=active.at[pl.ds(0, EDGE)],
            send_sem=edge_send.at[k],
            recv_sem=edge_recv.at[k],
            device_id=after,
            device_id_type=MESH,
        )
        down = pltpu.make_async_remote_copy(
            src_ref=active.at[pl.ds(EDGE, EDGE)],
            dst_ref=active.at[pl.ds(length + EDGE, EDGE)],
            send_sem=edge_send.at[k + 1],
            recv_sem=edge_recv.at[k + 1],
            device_id=before,
            device_id_type=MESH,
        )
        return up, down

    def depthwise(i, tile, tiles, active, taps, target):
        start = pl.multiple_of(i * tile, EDGE)

        @pl.loop(0, width // step)
        def _(n):
            columns = pl.ds(pl.multiple_of(n * step, 128), step)
            middle = active[pl.ds(pl.multiple_of(start + EDGE, EDGE), tile), columns].astype(
                jnp.float32
            )
            low = active[pl.ds(start, EDGE), columns].astype(jnp.float32)[EDGE - 1 :]
            high = active[
                pl.ds(pl.multiple_of(start + EDGE + tile, EDGE), EDGE), columns
            ].astype(jnp.float32)[:1]
            low = jnp.where((i == 0) & (slab == 0), 0.0, low)
            high = jnp.where((i == tiles - 1) & (slab == contexts - 1), 0.0, high)
            place = lax.broadcasted_iota(jnp.int32, middle.shape, 0)
            previous = jnp.where(place == 0, low, pltpu.roll(middle, 1, 0))
            following = jnp.where(place == tile - 1, high, pltpu.roll(middle, tile - 1, 0))
            tap = taps[:, columns].astype(jnp.float32)
            value = tap[0:1] * previous + tap[1:2] * middle + tap[2:3] * following
            target[me, pl.ds(start, tile), columns] = value.astype(jnp.bfloat16)

    def mix(i, tile, source, weight, target):
        rows = pl.ds(pl.multiple_of(i * tile, EDGE), tile)

        @pl.loop(0, width // step)
        def _(n):
            columns = pl.ds(pl.multiple_of(n * step, 128), step)
            total = jnp.zeros((tile, step), jnp.float32)
            for j in range(tensors):
                total += dot(source[j, rows], weight[pl.ds(j * width, width), columns])
            target[me, rows, columns] = total.astype(jnp.bfloat16)

    for k in (0, 1, 3, 4, 5):
        locals_[k].wait()
    g_trunk.arrived(0)
    g_skip_mid.arrived(0)
    g_skip_fine.start(0, skip_fine)

    @pl.loop(0, g_taps_mid.tiles)
    def _(i):
        project(
            i, tile_mid, trunk_all, skip_mid_all, w_coarse_mid, w_lateral_mid,
            gain_mid, shift_mid, active_mid,
        )

    edges_mid = edges(active_mid, 0)
    for copy in edges_mid:
        copy.start()
    for copy in edges_mid:
        copy.wait()

    @pl.loop(0, g_taps_mid.tiles)
    def _(i):
        depthwise(i, tile_mid, g_taps_mid.tiles, active_mid, depth_mid, taps_mid_all)
        g_taps_mid.start(i)

    cut = min(2, fine_tiles)
    for k in range(1, cut):
        g_skip_fine.start(k, skip_fine)

    @pl.loop(0, g_taps_mid.tiles)
    def _(i):
        g_taps_mid.arrived(i)
        mix(i, tile_mid, taps_mid_all, w_mixing_mid, hidden_mid_all)
        g_hidden_mid.start(i)

    for k in range(cut, fine_tiles):
        g_skip_fine.start(k, skip_fine)

    for k in (6, 7, 8, 9):
        locals_[k].wait()

    @pl.loop(0, g_hidden_mid.tiles)
    def _(i):
        g_hidden_mid.arrived(i)

    @pl.loop(0, fine_tiles)
    def _(i):
        g_skip_fine.arrived(i)
        project(
            i, tile_fine, hidden_mid_all, skip_fine_all, w_coarse_fine, w_lateral_fine,
            gain_fine, shift_fine, active_fine,
        )

    edges_fine = edges(active_fine, 2)
    for copy in edges_fine:
        copy.start()
    for copy in edges_fine:
        copy.wait()

    @pl.loop(0, fine_tiles)
    def _(i):
        depthwise(i, tile_fine, fine_tiles, active_fine, depth_fine, taps_fine_all)
        g_taps_fine.start(i)

    def cross(i):
        return pltpu.make_async_remote_copy(
            src_ref=own_all.at[me, g_own.rows(i)],
            dst_ref=partner_all.at[me, g_own.rows(i)],
            send_sem=mirror_send.at[i],
            recv_sem=mirror_recv.at[i],
            device_id=mirror,
            device_id_type=MESH,
        )

    @pl.loop(0, fine_tiles)
    def _(i):
        g_taps_fine.arrived(i)
        mix(i, tile_fine, taps_fine_all, w_mixing_fine, own_all)
        cross(i).start()
        g_own.start(i)

    @pl.loop(0, fine_tiles)
    def _(i):
        g_own.arrived(i)

    def write(k):
        rows = g_own.rows(k)
        return pltpu.make_async_copy(result.at[rows], out.at[0, rows], out_sem.at[k])

    def predict(k):
        rows = g_own.rows(fine_tiles - 1 - k)
        g_partner.arrived(k)
        for j in range(tensors):
            turned[j] = dot(reverser[...], partner_all[j, g_own.rows(k)]).astype(jnp.bfloat16)

        @pl.loop(0, tracks // 256)
        def _(n):
            columns = pl.ds(pl.multiple_of(n * 256, 256), 256)
            a = jnp.zeros((tile_fine, 256), jnp.float32)
            b = jnp.zeros((tile_fine, 256), jnp.float32)
            for j in range(tensors):
                depth = pl.ds(j * width, width)
                a += dot(own_all[j, rows], w_head[depth, columns])
                b += dot(turned[j], w_flipped[depth, columns])
            result[rows, columns] = mean_softplus(a, b).astype(jnp.bfloat16)

        write(fine_tiles - 1 - k).start()

    @pl.loop(0, fine_tiles + 1)
    def _(k):
        @pl.when(k < fine_tiles)
        def _():
            cross(k).wait_recv()
            g_partner.start(k)

        @pl.when(k > 0)
        def _():
            predict(k - 1)

    for gather in (
        g_trunk, g_skip_mid, g_skip_fine, g_taps_mid, g_hidden_mid, g_taps_fine, g_own, g_partner
    ):
        gather.sent()

    @pl.loop(0, fine_tiles)
    def _(i):
        cross(i).wait_send()
        write(i).wait()


def solution(mesh):
    tensors, contexts = mesh.shape["tensor"], mesh.shape["context"]

    def on_device(
        trunk_rows, skip_mid, skip_fine, coarse_mid, lateral_mid, gain_mid, shift_mid, depth_mid,
        mixing_mid, coarse_fine, lateral_fine, gain_fine, shift_fine, depth_fine, mixing_fine,
        head_weight,
    ):
        _, coarse_rows, width = trunk_rows.shape
        mid_rows, fine_rows = skip_mid.shape[1], skip_fine.shape[1]
        depth, tracks = head_weight.shape
        tile_mid, tile_fine = min(128, mid_rows), min(256, fine_rows)
        mid_tiles, fine_tiles = mid_rows // tile_mid, fine_rows // tile_fine
        peers = max(tensors - 1, 1)
        bf16 = jnp.bfloat16

        def everyone(rows):
            return pltpu.VMEM((tensors, rows, width), bf16)

        square = pltpu.VMEM((depth, width), bf16)
        semaphores = []
        for tiles in (
            1, 1, fine_tiles, mid_tiles, mid_tiles, fine_tiles, fine_tiles, fine_tiles
        ):
            semaphores += [pltpu.SemaphoreType.DMA((peers, tiles))] * 2
        anywhere = pl.BlockSpec(memory_space=pl.ANY)
        inside = pl.BlockSpec(memory_space=pltpu.VMEM)

        def body(*refs):
            kernel((tensors, contexts, tile_mid, tile_fine), *refs)

        macs = width * depth * (coarse_rows + 2 * mid_rows + mid_rows + 2 * fine_rows)
        macs += 2 * fine_rows * depth * tracks
        return pl.pallas_call(
            body,
            out_shape=jax.ShapeDtypeStruct((1, fine_rows, tracks), bf16),
            in_specs=[anywhere] * 10 + [inside] * 6,
            out_specs=anywhere,
            scratch_shapes=[
                everyone(coarse_rows),
                everyone(mid_rows),
                everyone(fine_rows),
                everyone(mid_rows),
                everyone(mid_rows),
                everyone(fine_rows),
                everyone(fine_rows),
                everyone(fine_rows),
                pltpu.VMEM((mid_rows + 2 * EDGE, width), bf16),
                pltpu.VMEM((fine_rows + 2 * EDGE, width), bf16),
                square, square, square, square, square, square,
                pltpu.VMEM((depth, tracks), bf16),
                pltpu.VMEM((depth, tracks), bf16),
                everyone(tile_fine),
                everyone(tile_fine),
                pltpu.VMEM((fine_rows, tracks), bf16),
                pltpu.VMEM((tile_fine, tile_fine // 2), bf16),
                pltpu.VMEM((tile_fine, tile_fine), bf16),
                pltpu.VMEM((256, 256), bf16),
                pltpu.SemaphoreType.DMA((10,)),
                pltpu.SemaphoreType.DMA((fine_tiles,)),
                *semaphores,
                pltpu.SemaphoreType.DMA((fine_tiles,)),
                pltpu.SemaphoreType.DMA((fine_tiles,)),
                pltpu.SemaphoreType.DMA((4,)),
                pltpu.SemaphoreType.DMA((4,)),
            ],
            compiler_params=pltpu.CompilerParams(
                collective_id=0, has_side_effects=True, vmem_limit_bytes=60 * 2**20
            ),
            cost_estimate=pl.CostEstimate(
                flops=2 * macs, bytes_accessed=32 * 2**20, transcendentals=6 * 2**20
            ),
            name="upsample_and_predict",
        )(
            trunk_rows, skip_mid, skip_fine, coarse_mid, lateral_mid, mixing_mid, coarse_fine,
            lateral_fine, mixing_fine, head_weight, gain_mid[None], shift_mid[None], depth_mid,
            gain_fine[None], shift_fine[None], depth_fine,
        )

    rows = P("strand", ("group", "context"), "tensor")
    weight, vector = P(None, "tensor"), P("tensor")
    section = (weight, weight, vector, vector, weight, weight)
    return jax.shard_map(
        on_device,
        mesh=mesh,
        in_specs=(rows, rows, rows, *section, *section, weight),
        out_specs=rows,
        check_vma=False,
    )
```

time: 485 us -> 231 us (0.48)
  Pallas kernels: 0 us -> 220 us
  waiting for transfers between devices: 199 us -> 0 us
  blocking collectives: 94.7 us -> 0 us
  local copies, waits for them, and re-layouts: 103 us -> 9.89 us
  matrix products: 57.8 us -> 0 us
  between operations: 13.7 us -> 0.01 us
  starting transfers between devices: 10.1 us -> 0 us
    pallas_call x0 -> x1, Pallas kernels: none -> 220 us  [on_device(): pl.pallas_call(body, out_shape=jax.ShapeDtypeStruct((1, fine_rows, tracks...]
    all_gather x7 -> x0, waiting for transfers between devices: 185 us -> none  [the longest x2 70.5 us: upsample_section(): lax.all_gather(depthwise, 'tensor', axis=1, tiled=True)]
    all_to_all x2 -> x0, blocking collectives: 81.7 us -> none  [the longest x1 41.6 us: on_device(): lax.all_to_all(crossed, 'context', split_axis=0, concat_axis=0, tiled=True)]
    dot_general x8 -> x0, matrix products: 57.8 us -> none  [contract(): return jnp.dot(portion, weight, preferred_element_type=jnp.float32)]
    rev x1 -> x0, local copies, waits for them, and re-layouts: 37.8 us -> none  [flip_tracks(): values.reshape(row_count, track_count // 2, 2)[:, :, ::-1]]
    reshape x5 -> x0, local copies, waits for them, and re-layouts: 29.8 us -> none  [the longest x3 20.9 us: flip_tracks(): values.reshape(row_count, track_count // 2, 2)[:, :, ::-1]]
    all_to_all x1 -> x0, local copies, waits for them, and re-layouts: 15.2 us -> none  [on_device(): lax.all_to_all(reordered, 'context', split_axis=0, concat_axis=0, tiled=T...]
    all_gather x1 -> x0, blocking collectives: 13 us -> none  [upsample_section(): lax.all_gather(coarse, 'tensor', axis=1, tiled=True)]
  transfers between devices with their start and end apart: 12 -> 0, of which waited for: 9 -> 0; matrix products, arithmetic and copies ran while one was open for 21% -> 0% of each run, Pallas kernels for 0% -> 0%
where the time goes in v2:
time: 231 us; the launch traced here: 230 us
  Pallas kernels  220 us (95%)
  local copies, waits for them, and re-layouts  9.89 us (4%)
    pallas_call x1, Pallas kernels, on_device(): pl.pallas_call(body, out_shape=jax.ShapeDtypeStruct((1, fine_rows, tracks...  220 us
    unnamed x1, local copies, waits for them, and re-layouts  4.79 us

profile of v2, /device:TPU:0, one launch (start us, length us, event | category | flops | bytes accessed | tf_op | source)
XLA Modules:
  0.0 230.3 jit_solution(16466094487698478023)
XLA Ops:
  0.0 1.3 broadcast_in_dim.12.refs_10_
  1.3 1.3 broadcast_in_dim.13.refs_11_
  2.6 1.3 broadcast_in_dim.14.refs_13_
  3.8 1.3 broadcast_in_dim.15.refs_14_
  5.1 220.4 %upsample_and_predict.1 = bf16[1,1024,2048]{2,1,0:T(8,128)(2,1)} custom-call(bf16[1,256,768]{2,1,0:T(8,128)(2,1)} %refs_0_.1, bf16[1,512,768]{2,1,0:T(8,128)(2,1)} %refs_1_.1, bf16[1,1024,768]{2,1,0:T(8,128)(2,1)} %refs_2_.1, bf16[1536,768]{1,0:T(8,128)(2,1)} %refs_3_.1, bf16[1536,768]{1,0:T(8,128)(2,1)} %refs_4_.1, bf16[1536,768]{1,0:T(8,128)(2,1)} %refs_5_.1, ...), custom_call_target="tpu_custom_call" | custom-call | flops 21944598528 | bytes 33554432 | tf_op jit(solution)/shard_map/upsample_and_predict/pallas_call | solution.py:397
  225.6 4.8 %copy.18 = bf16[1,1024,2048]{2,1,0:T(8,128)(2,1)} copy(bf16[1,1024,2048]{2,1,0:T(8,128)(2,1)} %upsample_and_predict.1) | data formatting | bytes 8388608

commit v3 on v2

--- a/solution.py
+++ b/solution.py
@@ -71,7 +71,7 @@
     active_mid, active_fine,
     w_coarse_mid, w_lateral_mid, w_mixing_mid, w_coarse_fine, w_lateral_fine, w_mixing_fine,
     w_head, w_flipped,
-    expanded, turned, result, doubler, reverser, swapper,
+    vectors, expanded, turned, result, doubler, reverser, swapper,
     local_sem, out_sem,
     s0, r0, s1, r1, s2, r2, s3, r3, s4, r4, s5, r5, s6, r6, s7, r7,
     mirror_send, mirror_recv, edge_send, edge_recv,
@@ -114,8 +114,8 @@
         pl.semaphore_signal(barrier, inc=1, device_id=target, device_id_type=MESH)
     pl.semaphore_wait(barrier, tensors + 2)
 
-    g_trunk = Gather(peers, trunk_all, trunk_all.shape[1], s0, r0)
-    g_skip_mid = Gather(peers, skip_mid_all, skip_mid_all.shape[1], s1, r1)
+    g_trunk = Gather(peers, trunk_all, tile_mid // 2, s0, r0)
+    g_skip_mid = Gather(peers, skip_mid_all, tile_mid, s1, r1)
     g_skip_fine = Gather(peers, skip_fine_all, tile_fine, s2, r2)
     g_taps_mid = Gather(peers, taps_mid_all, tile_mid, s3, r3)
     g_hidden_mid = Gather(peers, hidden_mid_all, tile_mid, s4, r4)
@@ -124,8 +124,12 @@
     g_partner = Gather(peers, partner_all, tile_fine, s7, r7)
     fine_tiles = g_own.tiles
 
-    g_trunk.start(0, trunk)
-    g_skip_mid.start(0, skip_mid)
+    for k in range(g_trunk.tiles):
+        g_trunk.start(k, trunk)
+        g_skip_mid.start(k, skip_mid)
+    g_skip_fine.start(0, skip_fine)
+    for k, vector in enumerate((gain_mid, shift_mid, gain_fine, shift_fine)):
+        vectors[k : k + 1] = vector[...].reshape(1, width)
 
     def iotas(shape):
         return (
@@ -158,7 +162,7 @@
                 jnp.bfloat16
             )
 
-    def project(i, tile, coarse, lateral, w_coarse, w_lateral, gain, shift, active):
+    def project(i, tile, coarse, lateral, w_coarse, w_lateral, k, active):
         half = pl.ds(pl.multiple_of(i * (tile // 2), EDGE), tile // 2)
         rows = pl.ds(pl.multiple_of(i * tile, EDGE), tile)
         for j in range(tensors):
@@ -174,7 +178,7 @@
                 depth = pl.ds(j * width, width)
                 total += dot(expanded[j, :tile], w_coarse[depth, columns])
                 total += dot(lateral[j, rows], w_lateral[depth, columns])
-            value = gelu(gain[:, columns] * total + shift[:, columns])
+            value = gelu(vectors[k : k + 1, columns] * total + vectors[k + 1 : k + 2, columns])
             active[pl.ds(pl.multiple_of(EDGE + i * tile, EDGE), tile), columns] = value.astype(
                 jnp.bfloat16
             )
@@ -234,34 +238,50 @@
 
     for k in (0, 1, 3, 4, 5):
         locals_[k].wait()
-    g_trunk.arrived(0)
-    g_skip_mid.arrived(0)
-    g_skip_fine.start(0, skip_fine)
-
-    @pl.loop(0, g_taps_mid.tiles)
-    def _(i):
+
+    def section(tiles, project_tile, taps_tile, active, k):
+        up, down = edges(active, k)
+        project_tile(0)
+        down.start()
+        project_tile(1)
+
+        @pl.loop(1, tiles - 1)
+        def _(i):
+            project_tile(i + 1)
+
+            @pl.when(i == tiles - 2)
+            def _():
+                up.start()
+
+            taps_tile(i)
+
+        down.wait_recv()
+        taps_tile(tiles - 1)
+        up.wait_recv()
+        taps_tile(0)
+        up.wait_send()
+        down.wait_send()
+
+    def project_mid(i):
+        g_trunk.arrived(i)
+        g_skip_mid.arrived(i)
         project(
-            i, tile_mid, trunk_all, skip_mid_all, w_coarse_mid, w_lateral_mid,
-            gain_mid, shift_mid, active_mid,
-        )
-
-    edges_mid = edges(active_mid, 0)
-    for copy in edges_mid:
-        copy.start()
-    for copy in edges_mid:
-        copy.wait()
-
-    @pl.loop(0, g_taps_mid.tiles)
-    def _(i):
+            i, tile_mid, trunk_all, skip_mid_all, w_coarse_mid, w_lateral_mid, 0, active_mid
+        )
+
+    def taps_mid(i):
         depthwise(i, tile_mid, g_taps_mid.tiles, active_mid, depth_mid, taps_mid_all)
         g_taps_mid.start(i)
+
+    section(g_taps_mid.tiles, project_mid, taps_mid, active_mid, 0)
 
     cut = min(2, fine_tiles)
     for k in range(1, cut):
         g_skip_fine.start(k, skip_fine)
 
     @pl.loop(0, g_taps_mid.tiles)
-    def _(i):
+    def _(n):
+        i = lax.rem(n + 1, g_taps_mid.tiles)
         g_taps_mid.arrived(i)
         mix(i, tile_mid, taps_mid_all, w_mixing_mid, hidden_mid_all)
         g_hidden_mid.start(i)
@@ -276,24 +296,18 @@
     def _(i):
         g_hidden_mid.arrived(i)
 
-    @pl.loop(0, fine_tiles)
-    def _(i):
+    def project_fine(i):
         g_skip_fine.arrived(i)
         project(
-            i, tile_fine, hidden_mid_all, skip_fine_all, w_coarse_fine, w_lateral_fine,
-            gain_fine, shift_fine, active_fine,
-        )
-
-    edges_fine = edges(active_fine, 2)
-    for copy in edges_fine:
-        copy.start()
-    for copy in edges_fine:
-        copy.wait()
-
-    @pl.loop(0, fine_tiles)
-    def _(i):
+            i, tile_fine, hidden_mid_all, skip_fine_all, w_coarse_fine, w_lateral_fine, 2,
+            active_fine,
+        )
+
+    def taps_fine(i):
         depthwise(i, tile_fine, fine_tiles, active_fine, depth_fine, taps_fine_all)
         g_taps_fine.start(i)
+
+    section(fine_tiles, project_fine, taps_fine, active_fine, 2)
 
     def cross(i):
         return pltpu.make_async_remote_copy(
@@ -306,7 +320,8 @@
         )
 
     @pl.loop(0, fine_tiles)
-    def _(i):
+    def _(n):
+        i = lax.rem(n + 1, fine_tiles)
         g_taps_fine.arrived(i)
         mix(i, tile_fine, taps_fine_all, w_mixing_fine, own_all)
         cross(i).start()
@@ -340,15 +355,17 @@
         write(fine_tiles - 1 - k).start()
 
     @pl.loop(0, fine_tiles + 1)
-    def _(k):
-        @pl.when(k < fine_tiles)
+    def _(n):
+        k = lax.rem(n + 1, fine_tiles)
+
+        @pl.when(n < fine_tiles)
         def _():
             cross(k).wait_recv()
             g_partner.start(k)
 
-        @pl.when(k > 0)
+        @pl.when(n > 0)
         def _():
-            predict(k - 1)
+            predict(lax.rem(n, fine_tiles))
 
     for gather in (
         g_trunk, g_skip_mid, g_skip_fine, g_taps_mid, g_hidden_mid, g_taps_fine, g_own, g_partner
@@ -383,7 +400,7 @@
         square = pltpu.VMEM((depth, width), bf16)
         semaphores = []
         for tiles in (
-            1, 1, fine_tiles, mid_tiles, mid_tiles, fine_tiles, fine_tiles, fine_tiles
+            mid_tiles, mid_tiles, fine_tiles, mid_tiles, mid_tiles, fine_tiles, fine_tiles, fine_tiles
         ):
             semaphores += [pltpu.SemaphoreType.DMA((peers, tiles))] * 2
         anywhere = pl.BlockSpec(memory_space=pl.ANY)
@@ -413,6 +430,7 @@
                 square, square, square, square, square, square,
                 pltpu.VMEM((depth, tracks), bf16),
                 pltpu.VMEM((depth, tracks), bf16),
+                pltpu.VMEM((4, width), jnp.float32),
                 everyone(tile_fine),
                 everyone(tile_fine),
                 pltpu.VMEM((fine_rows, tracks), bf16),
@@ -436,8 +454,8 @@
             name="upsample_and_predict",
         )(
             trunk_rows, skip_mid, skip_fine, coarse_mid, lateral_mid, mixing_mid, coarse_fine,
-            lateral_fine, mixing_fine, head_weight, gain_mid[None], shift_mid[None], depth_mid,
-            gain_fine[None], shift_fine[None], depth_fine,
+            lateral_fine, mixing_fine, head_weight, gain_mid, shift_mid, depth_mid,
+            gain_fine, shift_fine, depth_fine,
         )
 
     rows = P("strand", ("group", "context"), "tensor")

time: 231 us -> 217 us (0.939)
  Pallas kernels: 220 us -> 212 us
  local copies, waits for them, and re-layouts: 9.89 us -> 4.79 us
    pallas_call x1, Pallas kernels: 220 us -> 212 us  [on_device(): pl.pallas_call(body, out_shape=jax.ShapeDtypeStruct((1, fine_rows, tracks...]
    broadcast_in_dim x4 -> x0, local copies, waits for them, and re-layouts: 5.11 us -> none  [the longest x1 1.28 us: on_device(): shift_mid[None]]
where the time goes in v3:
time: 217 us; the launch traced here: 216 us
  Pallas kernels  212 us (98%)
  local copies, waits for them, and re-layouts  4.79 us (2%)
    pallas_call x1, Pallas kernels, on_device(): pl.pallas_call(body, out_shape=jax.ShapeDtypeStruct((1, fine_rows, tracks...  212 us
    unnamed x1, local copies, waits for them, and re-layouts  4.79 us

profile of v3, /device:TPU:0, one launch (start us, length us, event | category | flops | bytes accessed | tf_op | source)
XLA Modules:
  0.0 216.4 jit_solution(4626871850584241919)
XLA Ops:
  0.0 211.6 %upsample_and_predict.1 = bf16[1,1024,2048]{2,1,0:T(8,128)(2,1)} custom-call(bf16[1,256,768]{2,1,0:T(8,128)(2,1)} %refs_0_.1, bf16[1,512,768]{2,1,0:T(8,128)(2,1)} %refs_1_.1, bf16[1,1024,768]{2,1,0:T(8,128)(2,1)} %refs_2_.1, bf16[1536,768]{1,0:T(8,128)(2,1)} %refs_3_.1, bf16[1536,768]{1,0:T(8,128)(2,1)} %refs_4_.1, bf16[1536,768]{1,0:T(8,128)(2,1)} %refs_5_.1, ...), custom_call_target="tpu_custom_call" | custom-call | flops 21944598528 | bytes 33554432 | tf_op jit(solution)/shard_map/upsample_and_predict/pallas_call | solution.py:414
  211.6 4.8 %copy.18 = bf16[1,1024,2048]{2,1,0:T(8,128)(2,1)} copy(bf16[1,1024,2048]{2,1,0:T(8,128)(2,1)} %upsample_and_predict.1) | data formatting | bytes 8388608

commit v4 on v3

--- a/solution.py
+++ b/solution.py
@@ -127,7 +127,9 @@
     for k in range(g_trunk.tiles):
         g_trunk.start(k, trunk)
         g_skip_mid.start(k, skip_mid)
-    g_skip_fine.start(0, skip_fine)
+    first_cut, cut = max(1, fine_tiles // 4), max(1, fine_tiles // 2)
+    for k in range(first_cut):
+        g_skip_fine.start(k, skip_fine)
     for k, vector in enumerate((gain_mid, shift_mid, gain_fine, shift_fine)):
         vectors[k : k + 1] = vector[...].reshape(1, width)
 
@@ -275,8 +277,7 @@
 
     section(g_taps_mid.tiles, project_mid, taps_mid, active_mid, 0)
 
-    cut = min(2, fine_tiles)
-    for k in range(1, cut):
+    for k in range(first_cut, cut):
         g_skip_fine.start(k, skip_fine)
 
     @pl.loop(0, g_taps_mid.tiles)
@@ -389,7 +390,7 @@
         _, coarse_rows, width = trunk_rows.shape
         mid_rows, fine_rows = skip_mid.shape[1], skip_fine.shape[1]
         depth, tracks = head_weight.shape
-        tile_mid, tile_fine = min(128, mid_rows), min(256, fine_rows)
+        tile_mid, tile_fine = min(128, mid_rows), min(128, fine_rows)
         mid_tiles, fine_tiles = mid_rows // tile_mid, fine_rows // tile_fine
         peers = max(tensors - 1, 1)
         bf16 = jnp.bfloat16

time: 217 us -> 222 us (1.023)
  Pallas kernels: 212 us -> 217 us
    pallas_call x1, Pallas kernels: 212 us -> 217 us  [on_device(): pl.pallas_call(body, out_shape=jax.ShapeDtypeStruct((1, fine_rows, tracks...]
where the time goes in v4:
time: 222 us; the launch traced here: 221 us
  Pallas kernels  217 us (98%)
  local copies, waits for them, and re-layouts  4.79 us (2%)
    pallas_call x1, Pallas kernels, on_device(): pl.pallas_call(body, out_shape=jax.ShapeDtypeStruct((1, fine_rows, tracks...  217 us
    unnamed x1, local copies, waits for them, and re-layouts  4.79 us

profile of v4, /device:TPU:0, one launch (start us, length us, event | category | flops | bytes accessed | tf_op | source)
XLA Modules:
  0.0 221.3 jit_solution(10649819533375858430)
XLA Ops:
  0.0 216.5 %upsample_and_predict.1 = bf16[1,1024,2048]{2,1,0:T(8,128)(2,1)} custom-call(bf16[1,256,768]{2,1,0:T(8,128)(2,1)} %refs_0_.1, bf16[1,512,768]{2,1,0:T(8,128)(2,1)} %refs_1_.1, bf16[1,1024,768]{2,1,0:T(8,128)(2,1)} %refs_2_.1, bf16[1536,768]{1,0:T(8,128)(2,1)} %refs_3_.1, bf16[1536,768]{1,0:T(8,128)(2,1)} %refs_4_.1, bf16[1536,768]{1,0:T(8,128)(2,1)} %refs_5_.1, ...), custom_call_target="tpu_custom_call" | custom-call | flops 21944598528 | bytes 33554432 | tf_op jit(solution)/shard_map/upsample_and_predict/pallas_call | solution.py:415
  216.5 4.8 %copy.18 = bf16[1,1024,2048]{2,1,0:T(8,128)(2,1)} copy(bf16[1,1024,2048]{2,1,0:T(8,128)(2,1)} %upsample_and_predict.1) | data formatting | bytes 8388608
